TPU v7x, 128 devices: a whole 4x4x4 slice. The times are simulated.
128 devices in a mesh: row: 16 (over z, x_hi, core), col: 8 (over y, x_lo).
Axes of the slice: x: 4 (x_hi: 2, x_lo: 2; x = x_hi * 2 + x_lo), y: 4, z: 4, core: 2. Of those that a mesh axis runs over, the one named last changes fastest.
Arguments:
- matrix: bfloat16 [8192, 8192], P('row', 'col'), may hold values from -6 to 6
- factors: float32 [8192, 8192], P('row', 'col')
- inverse: bfloat16 [64, 128, 128], P('col'), may hold values from -0.007171631 to 0.007171631
- pattern: int32 [64, 64], P('row', 'col'), may hold values from 0 to 1, as said below
- dropped: int32 [64, 64], P('row', 'col'), may hold values from 0 to 1, as said below
Outputs:
- factors_out: float32 [8192, 8192], P('row', 'col')
Inputs may be any that keep to these rules, and one draw needn't show every extreme that they name: Block (I, J) can be in the pattern only where I - J is 0, 1, -1, 4, -4, 32 or -32; the blocks with I - J of 0, 1, -1, 4 and -4 are always in it. In each device's region of 4 block rows by 8 block columns, every block column holds at most 3 pattern blocks (exactly 3 in some columns), and every block row at most 2 pattern blocks below the block diagonal (exactly 2 in some rows). `dropped`: dropped blocks lie in the pattern and off the block diagonal.
All inputs are finite; a program needn't handle non-finite values.
Results may differ from a plain program's by a relative error of at most 0.00083.
Values may be sent and summed in bfloat16 or wider, within the bound.
No kernel may reach another device: no remote copies, remote signals or barrier semaphores. Data moves between devices by JAX's collectives and lax.ppermute only.
A program may use at most 128 MiB of HBM per device.

v0:
```python
import functools

import jax
import jax.numpy as jnp
from jax import lax
from jax.experimental import pallas as pl
from jax.experimental.pallas import tpu as pltpu
from jax.sharding import PartitionSpec as P

BS = 128
F32 = jnp.float32
BF16 = jnp.bfloat16

DIAG, RIGHT, LEFT, X, OFF = 0, 4, 7, 10, 11
SLOTS = 15


def role():
    r, c = lax.axis_index("row"), lax.axis_index("col")
    odd = lax.rem(r, 2)
    home = lax.div(r, 2)
    is_d = c == home
    is_n = jnp.where(odd == 1, c == home + 1, c == home - 1)
    is_f = jnp.where(r < 8, c == home + 4, c == home - 4)
    even = odd == 0
    return dict(
        odd=odd,
        even=even,
        d=is_d,
        n=is_n,
        f=is_f,
        near=is_d | is_n,
        any=is_d | is_n | is_f,
        late=r >= 8,
        lower=(is_d & (odd == 1)) | (is_n & even) | (is_f & (r >= 8)),
        first=4 * odd,
        off=jnp.where(is_f, 4 * odd, 4 * (1 - odd)),
        x_row=jnp.where(odd == 1, jnp.where(is_d, 0, 3), jnp.where(is_d, 3, 0)),
        x_col=jnp.where(odd == 1, jnp.where(is_d, 3, 0), jnp.where(is_d, 4, 7)),
    )


def places(w):
    out = []
    for j in range(4):
        out.append((DIAG + j, j, w["first"] + j, "d"))
    for j in range(3):
        out.append((RIGHT + j, j, w["first"] + j + 1, "d"))
    for j in range(3):
        out.append((LEFT + j, j + 1, w["first"] + j, "d"))
    out.append((X, w["x_row"], w["x_col"], "near"))
    for j in range(4):
        out.append((OFF + j, j, w["off"] + j, "any"))
    return out


def block(ref, i, c):
    return ref.at[pl.ds(pl.multiple_of(i * BS, BS), BS), pl.ds(pl.multiple_of(c * BS, BS), BS)]


def grouped(w, todo):
    for name in ("d", "near", "any"):
        some = [t for t in todo if t[0] == name]
        if some:

            @pl.when(w[name])
            def _():
                for _, act in some:
                    act()


def fetch_blocks(w, src, dst, sem, start):
    def act(slot, i, c):
        copy = pltpu.make_async_copy(block(src, i, c), dst.at[slot], sem)
        copy.start() if start else copy.wait()

    grouped(w, [(g, functools.partial(act, s, i, c)) for s, i, c, g in places(w)])


def masked(w, f, table):
    def act(slot, i, c):
        f[slot] = f[slot] * (table[i, c] == 1).astype(F32)

    grouped(w, [(g, functools.partial(act, s, i, c)) for s, i, c, g in places(w)])


def send_blocks(w, f, sa, sb, sc, sd):
    def put(dst, at, slot):
        dst[at] = f[slot].astype(BF16)

    def off_x(dst):
        for j in range(4):
            put(dst, j, OFF + j)
        put(dst, 4, X)

    def off(dst):
        for j in range(4):
            put(dst, j, OFF + j)

    def diag(dst):
        for j in range(4):
            put(dst, j, DIAG + j)

    @pl.when(w["d"])
    def _():
        diag(sc)

        @pl.when(w["even"])
        def _():
            off_x(sa)
            diag(sb)

        @pl.when(jnp.logical_not(w["even"]))
        def _():
            diag(sa)

    @pl.when(w["n"])
    def _():
        @pl.when(w["even"])
        def _():
            off_x(sb)

        @pl.when(jnp.logical_not(w["even"]))
        def _():
            off_x(sa)

    @pl.when(w["f"])
    def _():
        @pl.when(w["late"])
        def _():
            off(sd)

        @pl.when(jnp.logical_not(w["late"]))
        def _():
            off(sc)


def receive(w, ra, rb, rc, rd, lb, ub, ud, sem, start):
    def go(src, dst):
        copy = pltpu.make_async_copy(src, dst, sem)
        copy.start() if start else copy.wait()

    def middle(ref, j, k):
        return ref.at[j, pl.ds(k * BS, BS), :]

    def side(ref, j, k):
        return ref.at[j, :, pl.ds(k * BS, BS)]

    @pl.when(w["d"])
    def _():
        go(ra.at[4], middle(ub, 0, 0))
        for j in range(4):
            go(ra.at[j], middle(ub, j, 1))

        @pl.when(w["even"])
        def _():
            go(rb.at[4], side(lb, 0, 0))
            for j in range(4):
                go(rb.at[j], side(lb, j, 1))

        @pl.when(jnp.logical_not(w["even"]))
        def _():
            go(rb.at[pl.ds(0, 4)], ud)

        @pl.when(w["late"])
        def _():
            for j in range(4):
                go(rc.at[j], middle(ub, j, 2))
                go(rd.at[j], side(lb, j, 2))

    @pl.when(w["n"] & w["even"])
    def _():
        go(ra.at[pl.ds(0, 4)], ud)

    @pl.when(w["f"] & w["late"])
    def _():
        go(rc, ud)


def sweep(w, f, a, inv, table, lb, ub, ud):
    def member(i, c):
        return (table[i, c] == 1).astype(F32)

    def lower_update(slot, i, c, u, inv_block):
        old = f[slot]
        product = jnp.dot(old.astype(BF16), u, preferred_element_type=F32)
        residual = (a[slot].astype(F32) - product) * member(i, c)
        step = jnp.dot(residual.astype(BF16), inv_block, preferred_element_type=F32)
        f[slot] = old + step * member(i, c)

    def upper_update(slot, i, c):
        old = f[slot]
        f[slot] = old + (a[slot].astype(F32) - old) * member(i, c)

    spots = {s: (i, c) for s, i, c, _ in places(w)}

    @pl.when(w["d"])
    def _():
        for j in range(3):
            lb[j + 1, :, pl.ds(0, BS)] = f[LEFT + j].astype(BF16)
            ub[j + 1, pl.ds(0, BS), :] = f[RIGHT + j].astype(BF16)

        @pl.when(jnp.logical_not(w["even"]))
        def _():
            lb[0, :, pl.ds(0, BS)] = f[X].astype(BF16)
            for j in range(4):
                lb[j, :, pl.ds(BS, BS)] = f[OFF + j].astype(BF16)

        @pl.when(jnp.logical_not(w["late"]))
        def _():
            for j in range(4):
                lb[j, :, pl.ds(2 * BS, BS)] = jnp.zeros((BS, BS), BF16)
                ub[j, pl.ds(2 * BS, BS), :] = jnp.zeros((BS, BS), BF16)

        for j in range(3):
            lower_update(LEFT + j, *spots[LEFT + j], f[DIAG + j].astype(BF16), inv[w["first"] + j])
        for j in range(3):
            upper_update(RIGHT + j, *spots[RIGHT + j])
        for j in range(4):
            i, c = spots[DIAG + j]
            old = f[DIAG + j]
            product = jnp.dot(lb[j], ub[j], preferred_element_type=F32)
            residual = (a[DIAG + j].astype(F32) - product - old) * member(i, c)
            f[DIAG + j] = old + residual

    @pl.when(w["lower"])
    def _():
        for j in range(4):
            lower_update(OFF + j, *spots[OFF + j], ud[j], inv[w["off"] + j])

        @pl.when(w["near"])
        def _():
            lower_update(X, *spots[X], ud[3], inv[w["off"] + 3])

    @pl.when(w["any"] & jnp.logical_not(w["lower"]))
    def _():
        for j in range(4):
            upper_update(OFF + j, *spots[OFF + j])

        @pl.when(w["near"])
        def _():
            upper_update(X, *spots[X])


def first_kernel(pattern, factors, sa, sb, sc, sd, table, f, sem, table_sem):
    w = role()

    @pl.when(w["any"])
    def _():
        get_table = pltpu.make_async_copy(pattern, table, table_sem)
        get_table.start()
        fetch_blocks(w, factors, f, sem, True)
        get_table.wait()
        fetch_blocks(w, factors, f, sem, False)
        masked(w, f, table)
        send_blocks(w, f, sa, sb, sc, sd)


def middle_kernel(pattern, factors, matrix, inverse, ra, rb, rc, rd, sa, sb, sc, sd, state,
                  table, f, a, inv, lb, ub, ud, sems):
    w = role()

    @pl.when(w["any"])
    def _():
        get_table = pltpu.make_async_copy(pattern, table, sems.at[0])
        get_inv = pltpu.make_async_copy(inverse, inv, sems.at[1])
        get_table.start()
        fetch_blocks(w, factors, f, sems.at[2], True)
        receive(w, ra, rb, rc, rd, lb, ub, ud, sems.at[4], True)
        fetch_blocks(w, matrix, a, sems.at[3], True)
        get_inv.start()
        get_table.wait()
        fetch_blocks(w, factors, f, sems.at[2], False)
        masked(w, f, table)
        receive(w, ra, rb, rc, rd, lb, ub, ud, sems.at[4], False)
        fetch_blocks(w, matrix, a, sems.at[3], False)
        get_inv.wait()
        sweep(w, f, a, inv, table, lb, ub, ud)
        keep = pltpu.make_async_copy(f, state, sems.at[2])
        keep.start()
        send_blocks(w, f, sa, sb, sc, sd)
        keep.wait()


def zero_kernel(out, zeros, sem):
    zeros[...] = jnp.zeros_like(zeros)
    rows = zeros.shape[0]
    copies = [
        pltpu.make_async_copy(zeros, out.at[pl.ds(k * rows, rows)], sem)
        for k in range(out.shape[0] // rows)
    ]
    for copy in copies:
        copy.start()
    for copy in copies:
        copy.wait()


def last_kernel(pattern, dropped, matrix, inverse, state, ra, rb, rc, rd, zeroed, out,
                table, drops, f, a, inv, lb, ub, ud, sems):
    del zeroed
    w = role()

    @pl.when(w["any"])
    def _():
        get_table = pltpu.make_async_copy(pattern, table, sems.at[0])
        get_drops = pltpu.make_async_copy(dropped, drops, sems.at[5])
        get_inv = pltpu.make_async_copy(inverse, inv, sems.at[1])
        get_state = pltpu.make_async_copy(state, f, sems.at[2])
        get_table.start()
        get_drops.start()
        get_state.start()
        receive(w, ra, rb, rc, rd, lb, ub, ud, sems.at[4], True)
        fetch_blocks(w, matrix, a, sems.at[3], True)
        get_inv.start()
        get_table.wait()
        get_drops.wait()
        get_state.wait()
        receive(w, ra, rb, rc, rd, lb, ub, ud, sems.at[4], False)
        fetch_blocks(w, matrix, a, sems.at[3], False)
        get_inv.wait()
        sweep(w, f, a, inv, table, lb, ub, ud)

        def write(slot, i, c):
            f[slot] = f[slot] * (1 - drops[i, c]).astype(F32)
            pltpu.make_async_copy(f.at[slot], block(out, i, c), sems.at[2]).start()

        def done(slot, i, c):
            pltpu.make_async_copy(f.at[slot], block(out, i, c), sems.at[2]).wait()

        for act in (write, done):
            grouped(w, [(g, functools.partial(act, s, i, c)) for s, i, c, g in places(w)])


def routes(cols):
    def at(r, c):
        return r * cols + c

    a, b, c8, d = [], [], [], []
    for r in range(16):
        home = r // 2
        if r % 2 == 0:
            a.append((at(r, home), at(r + 1, home)))
            b.append((at(r, home), at(r + 1, home)))
            if r > 0:
                b.append((at(r, home - 1), at(r, home)))
        elif r < 15:
            a.append((at(r, home), at(r + 1, home)))
            a.append((at(r, home + 1), at(r + 1, home + 1)))
        if r < 8:
            c8.append((at(r, home), at(r + 8, home)))
            c8.append((at(r, home + 4), at(r + 8, home + 4)))
        else:
            d.append((at(r, home - 4), at(r, home)))
    return a, b, c8, d


def exchange(buffers):
    return [
        lax.ppermute(x, ("row", "col"), route)
        for x, route in zip(buffers, routes(lax.axis_size("col")))
    ]


ANY = pl.BlockSpec(memory_space=pl.ANY)
VM = pl.BlockSpec(memory_space=pltpu.VMEM)
SENT = [jax.ShapeDtypeStruct((n, BS, BS), BF16) for n in (5, 5, 4, 4)]
MIB = 1 << 20


def params():
    return pltpu.CompilerParams(vmem_limit_bytes=24 * MIB)


def on_device(matrix, factors, inverse, pattern, dropped):
    blocks = pltpu.VMEM((SLOTS, BS, BS), F32)
    halves = pltpu.VMEM((SLOTS, BS, BS), BF16)
    table = pltpu.SMEM(pattern.shape, jnp.int32)
    operands = [
        pltpu.VMEM(inverse.shape, BF16),
        pltpu.VMEM((4, BS, 3 * BS), BF16),
        pltpu.VMEM((4, 3 * BS, BS), BF16),
        pltpu.VMEM((4, BS, BS), BF16),
    ]
    sem = pltpu.SemaphoreType.DMA

    sent = pl.pallas_call(
        first_kernel,
        out_shape=SENT,
        in_specs=[ANY] * 2,
        out_specs=[VM] * 4,
        scratch_shapes=[table, blocks, sem, sem],
        compiler_params=params(),
        name="first",
    )(pattern, factors)
    got = exchange(sent)
    zeroed = pl.pallas_call(
        zero_kernel,
        out_shape=jax.ShapeDtypeStruct(factors.shape, F32),
        out_specs=ANY,
        scratch_shapes=[pltpu.VMEM((64, factors.shape[1]), F32), sem],
        compiler_params=params(),
        cost_estimate=pl.CostEstimate(flops=0, bytes_accessed=factors.size * 4, transcendentals=0),
        name="zeros",
    )()
    *sent, state = pl.pallas_call(
        middle_kernel,
        out_shape=[*SENT, jax.ShapeDtypeStruct((SLOTS, BS, BS), F32)],
        in_specs=[ANY] * 8,
        out_specs=[VM] * 4 + [ANY],
        scratch_shapes=[table, blocks, halves, *operands, pltpu.SemaphoreType.DMA((5,))],
        compiler_params=params(),
        name="middle",
    )(pattern, factors, matrix, inverse, *got)
    got = exchange(sent)
    return pl.pallas_call(
        last_kernel,
        out_shape=jax.ShapeDtypeStruct(factors.shape, F32),
        in_specs=[ANY] * 10,
        out_specs=ANY,
        scratch_shapes=[table, table, blocks, halves, *operands, pltpu.SemaphoreType.DMA((6,))],
        input_output_aliases={9: 0},
        compiler_params=params(),
        name="last",
    )(pattern, dropped, matrix, inverse, state, *got, zeroed)


def solution(mesh):
    placed = (
        P("row", "col"),
        P("row", "col"),
        P("col", None, None),
        P("row", "col"),
        P("row", "col"),
    )
    return jax.shard_map(
        on_device, mesh=mesh, in_specs=placed, out_specs=P("row", "col"), check_vma=False
    )
```

profile of v0, /device:TPU:80, one launch (start us, length us, event | category | flops | bytes accessed | tf_op | source)
XLA Modules:
  0.0 37.6 jit_solution(14622687369675303054)
XLA Ops:
  0.0 0.0 copy-start
  0.0 1.6 %copy-done = f32[512,1024]{1,0:T(8,128)S(1)} copy-done((f32[512,1024]{1,0:T(8,128)S(1)}, f32[512,1024]{1,0:T(8,128)}, u32[]{:S(2)}) %copy-start) | copy-done | bytes 2097176
  1.6 0.0 copy-start.3
  1.6 0.7 %copy-done.3 = s32[4,8]{1,0:T(4,128)S(1)} copy-done((s32[4,8]{1,0:T(4,128)S(1)}, s32[4,8]{1,0:T(4,128)}, u32[]{:S(2)}) %copy-start.3) | copy-done | bytes 152
  2.3 0.0 copy-start.1
  2.3 0.0 copy-start.2
  2.3 0.7 %first.1 = (bf16[5,128,128]{2,1,0:T(8,128)(2,1)S(1)}, bf16[5,128,128]{2,1,0:T(8,128)(2,1)S(1)}, bf16[4,128,128]{2,1,0:T(8,128)(2,1)S(1)}, bf16[4,128,128]{2,1,0:T(8,128)(2,1)S(1)}) custom-call(s32[4,8]{1,0:T(4,128)S(1)} %copy-done.3, f32[512,1024]{1,0:T(8,128)S(1)} %copy-done), custom_call_target="tpu_custom_call" | custom-call | tf_op jit(solution)/shard_map/first/pallas_call | solution.py:386
  3.0 1.9 %collective-permute-start = (bf16[5,128,128]{2,1,0:T(8,128)(2,1)S(1)}, bf16[5,128,128]{2,1,0:T(8,128)(2,1)S(1)}, u32[]{:S(2)}, u32[]{:S(2)}) collective-permute-start(bf16[5,128,128]{2,1,0:T(8,128)(2,1)S(1)} %get-tuple-element.14), channel_id=1, source_target_pairs={{0,8},{8,16},{9,17},{17,25},{25,33},{26,34},{34,42},{42,50},{43,51... | collective-permute-start | bytes 491528 | tf_op jit(solution)/shard_map/ppermute | solution.py:359
  4.9 5.0 %collective-permute-start.1 = (bf16[5,128,128]{2,1,0:T(8,128)(2,1)S(1)}, bf16[5,128,128]{2,1,0:T(8,128)(2,1)S(1)}, u32[]{:S(2)}, u32[]{:S(2)}) collective-permute-start(bf16[5,128,128]{2,1,0:T(8,128)(2,1)S(1)} %get-tuple-element.15), channel_id=1, source_target_pairs={{0,8},{17,25},{16,17},{34,42},{33,34},{51,59},{50,51},{68,76},{67,... | collective-permute-start | bytes 491528 | tf_op jit(solution)/shard_map/ppermute | solution.py:359
  9.9 1.3 %collective-permute-start.2 = (bf16[4,128,128]{2,1,0:T(8,128)(2,1)S(1)}, bf16[4,128,128]{2,1,0:T(8,128)(2,1)S(1)}, u32[]{:S(2)}, u32[]{:S(2)}) collective-permute-start(bf16[4,128,128]{2,1,0:T(8,128)(2,1)S(1)} %get-tuple-element.16), channel_id=1, source_target_pairs={{0,64},{4,68},{8,72},{12,76},{17,81},{21,85},{25,89},{29,93},{34,9... | collective-permute-start | bytes 393224 | tf_op jit(solution)/shard_map/ppermute | solution.py:359
  11.2 0.0 copy-start.4
  11.2 1.3 %collective-permute-start.3 = (bf16[4,128,128]{2,1,0:T(8,128)(2,1)S(1)}, bf16[4,128,128]{2,1,0:T(8,128)(2,1)S(1)}, u32[]{:S(2)}, u32[]{:S(2)}) collective-permute-start(bf16[4,128,128]{2,1,0:T(8,128)(2,1)S(1)} %get-tuple-element.17), channel_id=1, source_target_pairs={{64,68},{72,76},{81,85},{89,93},{98,102},{106,110},{115,119},{123,... | collective-permute-start | bytes 393224 | tf_op jit(solution)/shard_map/ppermute | solution.py:359
  12.5 5.8 %collective-permute-done.2.rc = bf16[4,128,128]{2,1,0:T(8,128)(2,1)S(1)} collective-permute-done((bf16[4,128,128]{2,1,0:T(8,128)(2,1)S(1)}, bf16[4,128,128]{2,1,0:T(8,128)(2,1)S(1)}, u32[]{:S(2)}, u32[]{:S(2)}) %collective-permute-start.2) | collective-permute-done | bytes 131104 | tf_op jit(solution)/shard_map/ppermute | solution.py:359
  18.3 1.3 %collective-permute-done.3.rd = bf16[4,128,128]{2,1,0:T(8,128)(2,1)S(1)} collective-permute-done((bf16[4,128,128]{2,1,0:T(8,128)(2,1)S(1)}, bf16[4,128,128]{2,1,0:T(8,128)(2,1)S(1)}, u32[]{:S(2)}, u32[]{:S(2)}) %collective-permute-start.3) | collective-permute-done | bytes 131104 | tf_op jit(solution)/shard_map/ppermute | solution.py:359
  19.6 0.0 collective-permute-done.ra
  19.6 0.0 collective-permute-done.1.rb
  19.6 0.0 copy-done.1
  19.6 0.0 copy-done.2
  19.6 1.9 %middle.1 = (bf16[5,128,128]{2,1,0:T(8,128)(2,1)S(1)}, bf16[5,128,128]{2,1,0:T(8,128)(2,1)S(1)}, bf16[4,128,128]{2,1,0:T(8,128)(2,1)S(1)}, bf16[4,128,128]{2,1,0:T(8,128)(2,1)S(1)}, f32[15,128,128]{2,1,0:T(8,128)S(1)}) custom-call(s32[4,8]{1,0:T(4,128)S(1)} %copy-done.3, f32[512,1024]{1,0:T(8,128)S(1)} %copy-done, bf16[512,1024]{1,0:T(8,128)(2,1)S(1)} %copy-done.1, ...), custom_call_target="tpu_custom_call" | custom-call | tf_op jit(solution)/shard_map/middle/pallas_call | solution.py:405
  21.6 1.9 %collective-permute-start.4 = (bf16[5,128,128]{2,1,0:T(8,128)(2,1)S(1)}, bf16[5,128,128]{2,1,0:T(8,128)(2,1)S(1)}, u32[]{:S(2)}, u32[]{:S(2)}) collective-permute-start(bf16[5,128,128]{2,1,0:T(8,128)(2,1)S(1)} %get-tuple-element.19), channel_id=1, source_target_pairs={{0,8},{8,16},{9,17},{17,25},{25,33},{26,34},{34,42},{42,50},{43,51... | collective-permute-start | bytes 491528 | tf_op jit(solution)/shard_map/ppermute | solution.py:359
  23.5 1.9 %collective-permute-start.5 = (bf16[5,128,128]{2,1,0:T(8,128)(2,1)S(1)}, bf16[5,128,128]{2,1,0:T(8,128)(2,1)S(1)}, u32[]{:S(2)}, u32[]{:S(2)}) collective-permute-start(bf16[5,128,128]{2,1,0:T(8,128)(2,1)S(1)} %get-tuple-element.20), channel_id=1, source_target_pairs={{0,8},{17,25},{16,17},{34,42},{33,34},{51,59},{50,51},{68,76},{67,... | collective-permute-start | bytes 491528 | tf_op jit(solution)/shard_map/ppermute | solution.py:359
  25.4 1.3 %collective-permute-start.6 = (bf16[4,128,128]{2,1,0:T(8,128)(2,1)S(1)}, bf16[4,128,128]{2,1,0:T(8,128)(2,1)S(1)}, u32[]{:S(2)}, u32[]{:S(2)}) collective-permute-start(bf16[4,128,128]{2,1,0:T(8,128)(2,1)S(1)} %get-tuple-element.21), channel_id=1, source_target_pairs={{0,64},{4,68},{8,72},{12,76},{17,81},{21,85},{25,89},{29,93},{34,9... | collective-permute-start | bytes 393224 | tf_op jit(solution)/shard_map/ppermute | solution.py:359
  26.7 1.3 %collective-permute-start.7 = (bf16[4,128,128]{2,1,0:T(8,128)(2,1)S(1)}, bf16[4,128,128]{2,1,0:T(8,128)(2,1)S(1)}, u32[]{:S(2)}, u32[]{:S(2)}) collective-permute-start(bf16[4,128,128]{2,1,0:T(8,128)(2,1)S(1)} %get-tuple-element.22), channel_id=1, source_target_pairs={{64,68},{72,76},{81,85},{89,93},{98,102},{106,110},{115,119},{123,... | collective-permute-start | bytes 393224 | tf_op jit(solution)/shard_map/ppermute | solution.py:359
  28.0 1.3 %zeros.1.zeroed = f32[512,1024]{1,0:T(8,128)} custom-call(), custom_call_target="tpu_custom_call" | custom-call | bytes 2097152 | tf_op jit(solution)/shard_map/zeros/pallas_call | solution.py:396
  29.4 4.4 %collective-permute-done.6.rc = bf16[4,128,128]{2,1,0:T(8,128)(2,1)S(1)} collective-permute-done((bf16[4,128,128]{2,1,0:T(8,128)(2,1)S(1)}, bf16[4,128,128]{2,1,0:T(8,128)(2,1)S(1)}, u32[]{:S(2)}, u32[]{:S(2)}) %collective-permute-start.6) | collective-permute-done | bytes 131104 | tf_op jit(solution)/shard_map/ppermute | solution.py:359
  33.8 1.3 %collective-permute-done.7.rd = bf16[4,128,128]{2,1,0:T(8,128)(2,1)S(1)} collective-permute-done((bf16[4,128,128]{2,1,0:T(8,128)(2,1)S(1)}, bf16[4,128,128]{2,1,0:T(8,128)(2,1)S(1)}, u32[]{:S(2)}, u32[]{:S(2)}) %collective-permute-start.7) | collective-permute-done | bytes 131104 | tf_op jit(solution)/shard_map/ppermute | solution.py:359
  35.1 0.0 collective-permute-done.4.ra
  35.1 0.0 collective-permute-done.5.rb
  35.1 0.0 copy-done.4
  35.1 2.5 %last.1 = f32[512,1024]{1,0:T(8,128)} custom-call(s32[4,8]{1,0:T(4,128)S(1)} %copy-done.3, s32[4,8]{1,0:T(4,128)S(1)} %copy-done.4, bf16[512,1024]{1,0:T(8,128)(2,1)S(1)} %copy-done.1, bf16[8,128,128]{2,1,0:T(8,128)(2,1)S(1)} %copy-done.2, f32[15,128,128]{2,1,0:T(8,128)S(1)} %get-tuple-element.18.state, ...), custom_call_target="tpu_custom_call", output_to_operand_aliasing={{}: (9, {})} | custom-call | tf_op jit(solution)/shard_map/last/pallas_call | solution.py:415
Async XLA Ops:
  0.0 1.6 %copy-start = (f32[512,1024]{1,0:T(8,128)S(1)}, f32[512,1024]{1,0:T(8,128)}, u32[]{:S(2)}) copy-start(f32[512,1024]{1,0:T(8,128)} %factors.3) | copy-start | bytes 6291460
  1.6 0.7 %copy-start.3 = (s32[4,8]{1,0:T(4,128)S(1)}, s32[4,8]{1,0:T(4,128)}, u32[]{:S(2)}) copy-start(s32[4,8]{1,0:T(4,128)} %pattern.5) | copy-start | bytes 388
  2.3 17.3 %copy-start.1 = (bf16[512,1024]{1,0:T(8,128)(2,1)S(1)}, bf16[512,1024]{1,0:T(8,128)(2,1)}, u32[]{:S(2)}) copy-start(bf16[512,1024]{1,0:T(8,128)(2,1)} %matrix.3) | copy-start | bytes 3145732
  2.3 17.3 %copy-start.2 = (bf16[8,128,128]{2,1,0:T(8,128)(2,1)S(1)}, bf16[8,128,128]{2,1,0:T(8,128)(2,1)}, u32[]{:S(2)}) copy-start(bf16[8,128,128]{2,1,0:T(8,128)(2,1)} %inverse.3) | copy-start | bytes 786436
  3.0 16.6 %collective-permute-start = (bf16[5,128,128]{2,1,0:T(8,128)(2,1)S(1)}, bf16[5,128,128]{2,1,0:T(8,128)(2,1)S(1)}, u32[]{:S(2)}, u32[]{:S(2)}) collective-permute-start(bf16[5,128,128]{2,1,0:T(8,128)(2,1)S(1)} %get-tuple-element.14), channel_id=1, source_target_pairs={{0,8},{8,16},{9,17},{17,25},{25,33},{26,34},{34,42},{42,50},{43,51... | collective-permute-start | bytes 491528 | tf_op jit(solution)/shard_map/ppermute | solution.py:359
  4.9 14.7 %collective-permute-start.1 = (bf16[5,128,128]{2,1,0:T(8,128)(2,1)S(1)}, bf16[5,128,128]{2,1,0:T(8,128)(2,1)S(1)}, u32[]{:S(2)}, u32[]{:S(2)}) collective-permute-start(bf16[5,128,128]{2,1,0:T(8,128)(2,1)S(1)} %get-tuple-element.15), channel_id=1, source_target_pairs={{0,8},{17,25},{16,17},{34,42},{33,34},{51,59},{50,51},{68,76},{67,... | collective-permute-start | bytes 491528 | tf_op jit(solution)/shard_map/ppermute | solution.py:359
  9.9 8.4 %collective-permute-start.2 = (bf16[4,128,128]{2,1,0:T(8,128)(2,1)S(1)}, bf16[4,128,128]{2,1,0:T(8,128)(2,1)S(1)}, u32[]{:S(2)}, u32[]{:S(2)}) collective-permute-start(bf16[4,128,128]{2,1,0:T(8,128)(2,1)S(1)} %get-tuple-element.16), channel_id=1, source_target_pairs={{0,64},{4,68},{8,72},{12,76},{17,81},{21,85},{25,89},{29,93},{34,9... | collective-permute-start | bytes 393224 | tf_op jit(solution)/shard_map/ppermute | solution.py:359
  11.2 23.9 %copy-start.4 = (s32[4,8]{1,0:T(4,128)S(1)}, s32[4,8]{1,0:T(4,128)}, u32[]{:S(2)}) copy-start(s32[4,8]{1,0:T(4,128)} %dropped.1) | copy-start | bytes 388
  11.2 8.4 %collective-permute-start.3 = (bf16[4,128,128]{2,1,0:T(8,128)(2,1)S(1)}, bf16[4,128,128]{2,1,0:T(8,128)(2,1)S(1)}, u32[]{:S(2)}, u32[]{:S(2)}) collective-permute-start(bf16[4,128,128]{2,1,0:T(8,128)(2,1)S(1)} %get-tuple-element.17), channel_id=1, source_target_pairs={{64,68},{72,76},{81,85},{89,93},{98,102},{106,110},{115,119},{123,... | collective-permute-start | bytes 393224 | tf_op jit(solution)/shard_map/ppermute | solution.py:359
  21.6 13.5 %collective-permute-start.4 = (bf16[5,128,128]{2,1,0:T(8,128)(2,1)S(1)}, bf16[5,128,128]{2,1,0:T(8,128)(2,1)S(1)}, u32[]{:S(2)}, u32[]{:S(2)}) collective-permute-start(bf16[5,128,128]{2,1,0:T(8,128)(2,1)S(1)} %get-tuple-element.19), channel_id=1, source_target_pairs={{0,8},{8,16},{9,17},{17,25},{25,33},{26,34},{34,42},{42,50},{43,51... | collective-permute-start | bytes 491528 | tf_op jit(solution)/shard_map/ppermute | solution.py:359
  23.5 11.6 %collective-permute-start.5 = (bf16[5,128,128]{2,1,0:T(8,128)(2,1)S(1)}, bf16[5,128,128]{2,1,0:T(8,128)(2,1)S(1)}, u32[]{:S(2)}, u32[]{:S(2)}) collective-permute-start(bf16[5,128,128]{2,1,0:T(8,128)(2,1)S(1)} %get-tuple-element.20), channel_id=1, source_target_pairs={{0,8},{17,25},{16,17},{34,42},{33,34},{51,59},{50,51},{68,76},{67,... | collective-permute-start | bytes 491528 | tf_op jit(solution)/shard_map/ppermute | solution.py:359
  25.4 8.4 %collective-permute-start.6 = (bf16[4,128,128]{2,1,0:T(8,128)(2,1)S(1)}, bf16[4,128,128]{2,1,0:T(8,128)(2,1)S(1)}, u32[]{:S(2)}, u32[]{:S(2)}) collective-permute-start(bf16[4,128,128]{2,1,0:T(8,128)(2,1)S(1)} %get-tuple-element.21), channel_id=1, source_target_pairs={{0,64},{4,68},{8,72},{12,76},{17,81},{21,85},{25,89},{29,93},{34,9... | collective-permute-start | bytes 393224 | tf_op jit(solution)/shard_map/ppermute | solution.py:359
  26.7 8.4 %collective-permute-start.7 = (bf16[4,128,128]{2,1,0:T(8,128)(2,1)S(1)}, bf16[4,128,128]{2,1,0:T(8,128)(2,1)S(1)}, u32[]{:S(2)}, u32[]{:S(2)}) collective-permute-start(bf16[4,128,128]{2,1,0:T(8,128)(2,1)S(1)} %get-tuple-element.22), channel_id=1, source_target_pairs={{64,68},{72,76},{81,85},{89,93},{98,102},{106,110},{115,119},{123,... | collective-permute-start | bytes 393224 | tf_op jit(solution)/shard_map/ppermute | solution.py:359
where the time goes:
time: 37.9 us; the launch traced here: 37.6 us
  starting transfers between devices  15.9 us (42%)
  waiting for transfers between devices  12.8 us (34%)
  Pallas kernels  6.49 us (17%)
  local copies, waits for them, and re-layouts  2.29 us (6%)
    ppermute x8, starting transfers between devices, exchange(): lax.ppermute(x, ('row', 'col'), route)  15.9 us
    ppermute x8, waiting for transfers between devices, exchange(): lax.ppermute(x, ('row', 'col'), route)  12.8 us
    pallas_call x1, Pallas kernels, on_device(): pl.pallas_call(last_kernel, out_shape=jax.ShapeDtypeStruct(factors.shape,...  2.5 us
    unnamed x10, local copies, waits for them, and re-layouts  2.29 us
    pallas_call x1, Pallas kernels, on_device(): pl.pallas_call(middle_kernel, out_shape=[*SENT, jax.ShapeDtypeStruct((SLO...  1.93 us
    pallas_call x1, Pallas kernels, on_device(): pl.pallas_call(zero_kernel, out_shape=jax.ShapeDtypeStruct(factors.shape,...  1.33 us
  transfers between devices with their start and end apart: 8, of which 4 were waited for; matrix products, arithmetic and copies ran while one was open for 0% of the time, Pallas kernels for 4%

commit v1 on v0

--- a/solution.py
+++ b/solution.py
@@ -2,6 +2,7 @@
 
 import jax
 import jax.numpy as jnp
+import numpy as np
 from jax import lax
 from jax.experimental import pallas as pl
 from jax.experimental.pallas import tpu as pltpu
@@ -128,11 +129,11 @@
     def _():
         @pl.when(w["late"])
         def _():
+            off(sc)
+
+        @pl.when(jnp.logical_not(w["late"]))
+        def _():
             off(sd)
-
-        @pl.when(jnp.logical_not(w["late"]))
-        def _():
-            off(sc)
 
 
 def receive(w, ra, rb, rc, rd, lb, ub, ud, sem, start):
@@ -165,8 +166,8 @@
         @pl.when(w["late"])
         def _():
             for j in range(4):
-                go(rc.at[j], middle(ub, j, 2))
-                go(rd.at[j], side(lb, j, 2))
+                go(rd.at[j], middle(ub, j, 2))
+                go(rc.at[j], side(lb, j, 2))
 
     @pl.when(w["n"] & w["even"])
     def _():
@@ -331,36 +332,86 @@
             grouped(w, [(g, functools.partial(act, s, i, c)) for s, i, c, g in places(w)])
 
 
-def routes(cols):
+def matched(cost):
+    n = len(cost)
+    u, v = np.zeros(n + 1), np.zeros(n + 1)
+    owner = np.zeros(n + 1, int)
+    for i in range(1, n + 1):
+        owner[0], j0 = i, 0
+        best = np.full(n + 1, np.inf)
+        back = np.zeros(n + 1, int)
+        used = np.zeros(n + 1, bool)
+        while owner[j0]:
+            used[j0] = True
+            i0 = owner[j0]
+            slack = cost[i0 - 1] - u[i0] - v[1:]
+            better = ~used[1:] & (slack < best[1:])
+            best[1:][better] = slack[better]
+            back[1:][better] = j0
+            j1 = int(np.argmin(np.where(used, np.inf, best)))
+            delta = best[j1]
+            u[owner[used]] += delta
+            v[used] -= delta
+            best[~used] -= delta
+            j0 = j1
+        while j0:
+            owner[j0] = owner[back[j0]]
+            j0 = back[j0]
+    return {int(owner[j]) - 1: j - 1 for j in range(1, n + 1)}
+
+
+def distance(a, b):
+    def chip(i):
+        r, c = divmod(i, 8)
+        return ((r // 2) % 2) * 2 + c % 2, c // 2, r // 4
+
+    return sum(min(abs(p - q), 4 - abs(p - q)) for p, q in zip(chip(a), chip(b)))
+
+
+def whole(pairs, busy):
+    sends, takes = {a for a, _ in pairs}, {b for _, b in pairs}
+    free_a = [i for i in range(128) if i not in sends]
+    free_b = [i for i in range(128) if i not in takes]
+
+    def price(a, b):
+        if a == b:
+            return 1e6
+        far = distance(a, b)
+        return (2 + far if far else 1) ** 2 * sum(10 if i in busy else 1 for i in (a, b))
+
+    pick = matched(np.array([[price(a, b) for b in free_b] for a in free_a], float))
+    return list(pairs) + [(a, free_b[pick[i]]) for i, a in enumerate(free_a)]
+
+
+def routes():
     def at(r, c):
-        return r * cols + c
-
-    a, b, c8, d = [], [], [], []
-    for r in range(16):
-        home = r // 2
-        if r % 2 == 0:
-            a.append((at(r, home), at(r + 1, home)))
-            b.append((at(r, home), at(r + 1, home)))
-            if r > 0:
-                b.append((at(r, home - 1), at(r, home)))
-        elif r < 15:
-            a.append((at(r, home), at(r + 1, home)))
-            a.append((at(r, home + 1), at(r + 1, home + 1)))
-        if r < 8:
-            c8.append((at(r, home), at(r + 8, home)))
-            c8.append((at(r, home + 4), at(r + 8, home + 4)))
-        else:
-            d.append((at(r, home - 4), at(r, home)))
-    return a, b, c8, d
+        return r * 8 + c
+
+    diag = [at(r, r // 2) for r in range(16)]
+    near = {r: at(r, r // 2 + (1 if r % 2 else -1)) for r in range(1, 15)}
+    far = [at(r, r // 2 + (4 if r < 8 else -4)) for r in range(16)]
+    busy = {*diag, *near.values(), *far}
+    pair = [(diag[r], diag[r + 1]) for r in range(0, 16, 2)]
+    a = pair + [(diag[r], near[r + 1]) for r in range(1, 14, 2)]
+    a += [(near[r], diag[r + 1]) for r in range(1, 14, 2)]
+    b = pair + [(near[r], diag[r]) for r in range(2, 15, 2)]
+    c, d = [], []
+    for r in range(8):
+        ring = [diag[r], far[r + 8], diag[r + 8], far[r]]
+        c += list(zip(ring, ring[1:] + ring[:1]))
+        d += [(far[r], diag[r + 8]), (diag[r + 8], far[r])]
+    return [whole(x, busy) for x in (a, b, c, d)]
 
 
 def exchange(buffers):
-    return [
-        lax.ppermute(x, ("row", "col"), route)
-        for x, route in zip(buffers, routes(lax.axis_size("col")))
-    ]
-
-
+    out = [None] * 4
+    for k in ORDER:
+        out[k] = lax.ppermute(buffers[k], ("row", "col"), ROUTES[k])
+    return out
+
+
+ROUTES = routes()
+ORDER = (1, 0, 2, 3)
 ANY = pl.BlockSpec(memory_space=pl.ANY)
 VM = pl.BlockSpec(memory_space=pltpu.VMEM)
 SENT = [jax.ShapeDtypeStruct((n, BS, BS), BF16) for n in (5, 5, 4, 4)]

time: 37.9 us -> 29.6 us (0.78)
  the two profiles are of different devices: /device:TPU:80 before, /device:TPU:16 now
where the time goes in v1:
time: 29.6 us; the launch traced here: 29.5 us
  waiting for transfers between devices  11.4 us (39%)
  starting transfers between devices  11.2 us (38%)
  Pallas kernels  4.56 us (15%)
  local copies, waits for them, and re-layouts  2.28 us (8%)
    ppermute x8, waiting for transfers between devices, exchange(): out[k] = lax.ppermute(buffers[k], ('row', 'col'), ROUTES[k])  11.4 us
    ppermute x8, starting transfers between devices, exchange(): out[k] = lax.ppermute(buffers[k], ('row', 'col'), ROUTES[k])  11.2 us
    unnamed x10, local copies, waits for them, and re-layouts  2.28 us
    pallas_call x1, Pallas kernels, on_device(): pl.pallas_call(last_kernel, out_shape=jax.ShapeDtypeStruct(factors.shape,...  1.44 us
    pallas_call x1, Pallas kernels, on_device(): pl.pallas_call(zero_kernel, out_shape=jax.ShapeDtypeStruct(factors.shape,...  1.33 us
    pallas_call x1, Pallas kernels, on_device(): pl.pallas_call(middle_kernel, out_shape=[*SENT, jax.ShapeDtypeStruct((SLO...  1.14 us
    pallas_call x1, Pallas kernels, on_device(): pl.pallas_call(first_kernel, out_shape=SENT, in_specs=[ANY] * 2, out_spec...  0.65 us
  transfers between devices with their start and end apart: 8, of which 4 were waited for; matrix products, arithmetic and copies ran while one was open for 0% of the time, Pallas kernels for 4%

profile of v1, /device:TPU:16, one launch (start us, length us, event | category | flops | bytes accessed | tf_op | source)
XLA Modules:
  0.0 29.5 jit_solution(16300789444529588425)
XLA Ops:
  0.0 0.0 copy-start
  0.0 1.6 %copy-done = f32[512,1024]{1,0:T(8,128)S(1)} copy-done((f32[512,1024]{1,0:T(8,128)S(1)}, f32[512,1024]{1,0:T(8,128)}, u32[]{:S(2)}) %copy-start) | copy-done | bytes 2097176
  1.6 0.0 copy-start.3
  1.6 0.7 %copy-done.3 = s32[4,8]{1,0:T(4,128)S(1)} copy-done((s32[4,8]{1,0:T(4,128)S(1)}, s32[4,8]{1,0:T(4,128)}, u32[]{:S(2)}) %copy-start.3) | copy-done | bytes 152
  2.3 0.0 copy-start.1
  2.3 0.0 copy-start.2
  2.3 0.7 %first.1 = (bf16[5,128,128]{2,1,0:T(8,128)(2,1)S(1)}, bf16[5,128,128]{2,1,0:T(8,128)(2,1)S(1)}, bf16[4,128,128]{2,1,0:T(8,128)(2,1)S(1)}, bf16[4,128,128]{2,1,0:T(8,128)(2,1)S(1)}) custom-call(s32[4,8]{1,0:T(4,128)S(1)} %copy-done.3, f32[512,1024]{1,0:T(8,128)S(1)} %copy-done), custom_call_target="tpu_custom_call" | custom-call | tf_op jit(solution)/shard_map/first/pallas_call | solution.py:437
  2.9 0.1 collective-permute-start
  3.0 0.5 %collective-permute-start.1 = (bf16[5,128,128]{2,1,0:T(8,128)(2,1)S(1)}, bf16[5,128,128]{2,1,0:T(8,128)(2,1)S(1)}, u32[]{:S(2)}, u32[]{:S(2)}) collective-permute-start(bf16[5,128,128]{2,1,0:T(8,128)(2,1)S(1)} %get-tuple-element.15), channel_id=1, source_target_pairs={{0,8},{17,25},{34,42},{51,59},{68,76},{85,93},{102,110},{119,127},... | collective-permute-start | bytes 491528 | tf_op jit(solution)/shard_map/ppermute | solution.py:409
  3.5 3.0 %collective-permute-start.2 = (bf16[4,128,128]{2,1,0:T(8,128)(2,1)S(1)}, bf16[4,128,128]{2,1,0:T(8,128)(2,1)S(1)}, u32[]{:S(2)}, u32[]{:S(2)}) collective-permute-start(bf16[4,128,128]{2,1,0:T(8,128)(2,1)S(1)} %get-tuple-element.16), channel_id=1, source_target_pairs={{0,64},{64,68},{68,4},{4,0},{8,72},{72,76},{76,12},{12,8},{17,81},... | collective-permute-start | bytes 393224 | tf_op jit(solution)/shard_map/ppermute | solution.py:409
  6.5 0.0 copy-start.4
  6.5 3.5 %collective-permute-start.3 = (bf16[4,128,128]{2,1,0:T(8,128)(2,1)S(1)}, bf16[4,128,128]{2,1,0:T(8,128)(2,1)S(1)}, u32[]{:S(2)}, u32[]{:S(2)}) collective-permute-start(bf16[4,128,128]{2,1,0:T(8,128)(2,1)S(1)} %get-tuple-element.17), channel_id=1, source_target_pairs={{4,68},{68,4},{12,76},{76,12},{21,85},{85,21},{29,93},{93,29},{38,... | collective-permute-start | bytes 393224 | tf_op jit(solution)/shard_map/ppermute | solution.py:409
  10.0 4.3 %collective-permute-done.2.rc = bf16[4,128,128]{2,1,0:T(8,128)(2,1)S(1)} collective-permute-done((bf16[4,128,128]{2,1,0:T(8,128)(2,1)S(1)}, bf16[4,128,128]{2,1,0:T(8,128)(2,1)S(1)}, u32[]{:S(2)}, u32[]{:S(2)}) %collective-permute-start.2) | collective-permute-done | bytes 131104 | tf_op jit(solution)/shard_map/ppermute | solution.py:409
  14.3 2.2 %collective-permute-done.3.rd = bf16[4,128,128]{2,1,0:T(8,128)(2,1)S(1)} collective-permute-done((bf16[4,128,128]{2,1,0:T(8,128)(2,1)S(1)}, bf16[4,128,128]{2,1,0:T(8,128)(2,1)S(1)}, u32[]{:S(2)}, u32[]{:S(2)}) %collective-permute-start.3) | collective-permute-done | bytes 131104 | tf_op jit(solution)/shard_map/ppermute | solution.py:409
  16.5 0.0 collective-permute-done.ra
  16.5 0.0 collective-permute-done.1.rb
  16.5 0.0 copy-done.1
  16.5 0.0 copy-done.2
  16.5 1.1 %middle.1 = (bf16[5,128,128]{2,1,0:T(8,128)(2,1)S(1)}, bf16[5,128,128]{2,1,0:T(8,128)(2,1)S(1)}, bf16[4,128,128]{2,1,0:T(8,128)(2,1)S(1)}, bf16[4,128,128]{2,1,0:T(8,128)(2,1)S(1)}, f32[15,128,128]{2,1,0:T(8,128)S(1)}) custom-call(s32[4,8]{1,0:T(4,128)S(1)} %copy-done.3, f32[512,1024]{1,0:T(8,128)S(1)} %copy-done, bf16[512,1024]{1,0:T(8,128)(2,1)S(1)} %copy-done.1, ...), custom_call_target="tpu_custom_call" | custom-call | tf_op jit(solution)/shard_map/middle/pallas_call | solution.py:456
  17.7 0.1 collective-permute-start.4
  17.7 0.5 %collective-permute-start.5 = (bf16[5,128,128]{2,1,0:T(8,128)(2,1)S(1)}, bf16[5,128,128]{2,1,0:T(8,128)(2,1)S(1)}, u32[]{:S(2)}, u32[]{:S(2)}) collective-permute-start(bf16[5,128,128]{2,1,0:T(8,128)(2,1)S(1)} %get-tuple-element.20), channel_id=1, source_target_pairs={{0,8},{17,25},{34,42},{51,59},{68,76},{85,93},{102,110},{119,127},... | collective-permute-start | bytes 491528 | tf_op jit(solution)/shard_map/ppermute | solution.py:409
  18.2 0.0 collective-permute-start.6
  18.2 3.5 %collective-permute-start.7 = (bf16[4,128,128]{2,1,0:T(8,128)(2,1)S(1)}, bf16[4,128,128]{2,1,0:T(8,128)(2,1)S(1)}, u32[]{:S(2)}, u32[]{:S(2)}) collective-permute-start(bf16[4,128,128]{2,1,0:T(8,128)(2,1)S(1)} %get-tuple-element.22), channel_id=1, source_target_pairs={{4,68},{68,4},{12,76},{76,12},{21,85},{85,21},{29,93},{93,29},{38,... | collective-permute-start | bytes 393224 | tf_op jit(solution)/shard_map/ppermute | solution.py:409
  21.8 1.3 %zeros.1.zeroed = f32[512,1024]{1,0:T(8,128)} custom-call(), custom_call_target="tpu_custom_call" | custom-call | bytes 2097152 | tf_op jit(solution)/shard_map/zeros/pallas_call | solution.py:447
  23.1 3.0 %collective-permute-done.6.rc = bf16[4,128,128]{2,1,0:T(8,128)(2,1)S(1)} collective-permute-done((bf16[4,128,128]{2,1,0:T(8,128)(2,1)S(1)}, bf16[4,128,128]{2,1,0:T(8,128)(2,1)S(1)}, u32[]{:S(2)}, u32[]{:S(2)}) %collective-permute-start.6) | collective-permute-done | bytes 131104 | tf_op jit(solution)/shard_map/ppermute | solution.py:409
  26.1 1.9 %collective-permute-done.7.rd = bf16[4,128,128]{2,1,0:T(8,128)(2,1)S(1)} collective-permute-done((bf16[4,128,128]{2,1,0:T(8,128)(2,1)S(1)}, bf16[4,128,128]{2,1,0:T(8,128)(2,1)S(1)}, u32[]{:S(2)}, u32[]{:S(2)}) %collective-permute-start.7) | collective-permute-done | bytes 131104 | tf_op jit(solution)/shard_map/ppermute | solution.py:409
  28.0 0.0 collective-permute-done.4.ra
  28.0 0.0 collective-permute-done.5.rb
  28.0 0.0 copy-done.4
  28.0 1.4 %last.1 = f32[512,1024]{1,0:T(8,128)} custom-call(s32[4,8]{1,0:T(4,128)S(1)} %copy-done.3, s32[4,8]{1,0:T(4,128)S(1)} %copy-done.4, bf16[512,1024]{1,0:T(8,128)(2,1)S(1)} %copy-done.1, bf16[8,128,128]{2,1,0:T(8,128)(2,1)S(1)} %copy-done.2, f32[15,128,128]{2,1,0:T(8,128)S(1)} %get-tuple-element.18.state, ...), custom_call_target="tpu_custom_call", output_to_operand_aliasing={{}: (9, {})} | custom-call | tf_op jit(solution)/shard_map/last/pallas_call | solution.py:466
Async XLA Ops:
  0.0 1.6 %copy-start = (f32[512,1024]{1,0:T(8,128)S(1)}, f32[512,1024]{1,0:T(8,128)}, u32[]{:S(2)}) copy-start(f32[512,1024]{1,0:T(8,128)} %factors.3) | copy-start | bytes 6291460
  1.6 0.7 %copy-start.3 = (s32[4,8]{1,0:T(4,128)S(1)}, s32[4,8]{1,0:T(4,128)}, u32[]{:S(2)}) copy-start(s32[4,8]{1,0:T(4,128)} %pattern.5) | copy-start | bytes 388
  2.3 14.2 %copy-start.1 = (bf16[512,1024]{1,0:T(8,128)(2,1)S(1)}, bf16[512,1024]{1,0:T(8,128)(2,1)}, u32[]{:S(2)}) copy-start(bf16[512,1024]{1,0:T(8,128)(2,1)} %matrix.3) | copy-start | bytes 3145732
  2.3 14.2 %copy-start.2 = (bf16[8,128,128]{2,1,0:T(8,128)(2,1)S(1)}, bf16[8,128,128]{2,1,0:T(8,128)(2,1)}, u32[]{:S(2)}) copy-start(bf16[8,128,128]{2,1,0:T(8,128)(2,1)} %inverse.3) | copy-start | bytes 786436
  2.9 13.6 %collective-permute-start = (bf16[5,128,128]{2,1,0:T(8,128)(2,1)S(1)}, bf16[5,128,128]{2,1,0:T(8,128)(2,1)S(1)}, u32[]{:S(2)}, u32[]{:S(2)}) collective-permute-start(bf16[5,128,128]{2,1,0:T(8,128)(2,1)S(1)} %get-tuple-element.14), channel_id=1, source_target_pairs={{0,8},{17,25},{34,42},{51,59},{68,76},{85,93},{102,110},{119,127},... | collective-permute-start | bytes 491528 | tf_op jit(solution)/shard_map/ppermute | solution.py:409
  3.0 13.5 %collective-permute-start.1 = (bf16[5,128,128]{2,1,0:T(8,128)(2,1)S(1)}, bf16[5,128,128]{2,1,0:T(8,128)(2,1)S(1)}, u32[]{:S(2)}, u32[]{:S(2)}) collective-permute-start(bf16[5,128,128]{2,1,0:T(8,128)(2,1)S(1)} %get-tuple-element.15), channel_id=1, source_target_pairs={{0,8},{17,25},{34,42},{51,59},{68,76},{85,93},{102,110},{119,127},... | collective-permute-start | bytes 491528 | tf_op jit(solution)/shard_map/ppermute | solution.py:409
  3.5 10.8 %collective-permute-start.2 = (bf16[4,128,128]{2,1,0:T(8,128)(2,1)S(1)}, bf16[4,128,128]{2,1,0:T(8,128)(2,1)S(1)}, u32[]{:S(2)}, u32[]{:S(2)}) collective-permute-start(bf16[4,128,128]{2,1,0:T(8,128)(2,1)S(1)} %get-tuple-element.16), channel_id=1, source_target_pairs={{0,64},{64,68},{68,4},{4,0},{8,72},{72,76},{76,12},{12,8},{17,81},... | collective-permute-start | bytes 393224 | tf_op jit(solution)/shard_map/ppermute | solution.py:409
  6.5 21.6 %copy-start.4 = (s32[4,8]{1,0:T(4,128)S(1)}, s32[4,8]{1,0:T(4,128)}, u32[]{:S(2)}) copy-start(s32[4,8]{1,0:T(4,128)} %dropped.1) | copy-start | bytes 388
  6.5 10.0 %collective-permute-start.3 = (bf16[4,128,128]{2,1,0:T(8,128)(2,1)S(1)}, bf16[4,128,128]{2,1,0:T(8,128)(2,1)S(1)}, u32[]{:S(2)}, u32[]{:S(2)}) collective-permute-start(bf16[4,128,128]{2,1,0:T(8,128)(2,1)S(1)} %get-tuple-element.17), channel_id=1, source_target_pairs={{4,68},{68,4},{12,76},{76,12},{21,85},{85,21},{29,93},{93,29},{38,... | collective-permute-start | bytes 393224 | tf_op jit(solution)/shard_map/ppermute | solution.py:409
  17.7 10.4 %collective-permute-start.4 = (bf16[5,128,128]{2,1,0:T(8,128)(2,1)S(1)}, bf16[5,128,128]{2,1,0:T(8,128)(2,1)S(1)}, u32[]{:S(2)}, u32[]{:S(2)}) collective-permute-start(bf16[5,128,128]{2,1,0:T(8,128)(2,1)S(1)} %get-tuple-element.19), channel_id=1, source_target_pairs={{0,8},{17,25},{34,42},{51,59},{68,76},{85,93},{102,110},{119,127},... | collective-permute-start | bytes 491528 | tf_op jit(solution)/shard_map/ppermute | solution.py:409
  17.7 10.3 %collective-permute-start.5 = (bf16[5,128,128]{2,1,0:T(8,128)(2,1)S(1)}, bf16[5,128,128]{2,1,0:T(8,128)(2,1)S(1)}, u32[]{:S(2)}, u32[]{:S(2)}) collective-permute-start(bf16[5,128,128]{2,1,0:T(8,128)(2,1)S(1)} %get-tuple-element.20), channel_id=1, source_target_pairs={{0,8},{17,25},{34,42},{51,59},{68,76},{85,93},{102,110},{119,127},... | collective-permute-start | bytes 491528 | tf_op jit(solution)/shard_map/ppermute | solution.py:409
  18.2 7.9 %collective-permute-start.6 = (bf16[4,128,128]{2,1,0:T(8,128)(2,1)S(1)}, bf16[4,128,128]{2,1,0:T(8,128)(2,1)S(1)}, u32[]{:S(2)}, u32[]{:S(2)}) collective-permute-start(bf16[4,128,128]{2,1,0:T(8,128)(2,1)S(1)} %get-tuple-element.21), channel_id=1, source_target_pairs={{0,64},{64,68},{68,4},{4,0},{8,72},{72,76},{76,12},{12,8},{17,81},... | collective-permute-start | bytes 393224 | tf_op jit(solution)/shard_map/ppermute | solution.py:409
  18.2 9.8 %collective-permute-start.7 = (bf16[4,128,128]{2,1,0:T(8,128)(2,1)S(1)}, bf16[4,128,128]{2,1,0:T(8,128)(2,1)S(1)}, u32[]{:S(2)}, u32[]{:S(2)}) collective-permute-start(bf16[4,128,128]{2,1,0:T(8,128)(2,1)S(1)} %get-tuple-element.22), channel_id=1, source_target_pairs={{4,68},{68,4},{12,76},{76,12},{21,85},{85,21},{29,93},{93,29},{38,... | collective-permute-start | bytes 393224 | tf_op jit(solution)/shard_map/ppermute | solution.py:409
